TPU v7x, 512 devices: a whole 4x8x8 slice. The times are simulated.
512 devices in a mesh: seq: 32 (over z, x), dp: 2 (over core), tensor: 8 (over y).
Axes of the slice: x: 4, y: 8, z: 8, core: 2. Of those that a mesh axis runs over, the one named last changes fastest.
Arguments:
- head_inputs: bfloat16 [2, 2560, 16384], P('dp', 'tensor', 'seq'), may hold values from -6 to 6
- b_proj: bfloat16 [2, 16384, 128], P('dp', 'seq'), may hold values from -0.59765625 to 0.59765625
- c_proj: bfloat16 [2, 16384, 128], P('dp', 'seq'), may hold values from -0.59765625 to 0.59765625
- dt_raw: float32 [2, 40, 16384], P('dp', 'tensor', 'seq'), may hold values from -2 to 0
- a_log: float32 [40], P('tensor'), as said below
- d_skip: float32 [40], P('tensor'), may hold values from 0.5 to 1.5
- w_out: bfloat16 [2560, 2560], P('tensor', 'dp'), may hold values from -0.125 to 0.125
- out_grad: bfloat16 [2, 2560, 16384], P('dp', 'tensor', 'seq'), may hold values from -6 to 6
Outputs:
- mixed: bfloat16 [2, 2560, 16384], P('dp', 'tensor', 'seq')
- grad_inputs: bfloat16 [2, 2560, 16384], P('dp', 'tensor', 'seq')
- grad_b: bfloat16 [2, 16384, 128], P('dp', 'seq')
- grad_c: bfloat16 [2, 16384, 128], P('dp', 'seq')
- grad_dt: float32 [2, 40, 16384], P('dp', 'tensor', 'seq')
- grad_alog: float32 [40], P('tensor')
- grad_skip: float32 [40], P('tensor')
- grad_w: bfloat16 [2560, 2560], P('tensor', ('seq', 'dp'))
Inputs may be any that keep to these rules, and one draw needn't show every extreme that they name: exp(a_log) lies between 0.1 / 16384 and 0.1.
All inputs are finite; a program needn't handle non-finite values.
Results may differ from a plain program's by a relative error of at most 0.0049.
Values may be sent and summed in bfloat16 or wider, within the bound.
A program may use at most 128 MiB of HBM per device.

v0:
```python
import jax
import jax.numpy as jnp
from jax import lax
from jax.sharding import PartitionSpec as P

SPAN = 256
HIGH = lax.Precision.HIGHEST


def span_pass(carried, x_block, b_block, c_block, step_block, decay_rate):
    log_decay = step_block * decay_rate[:, None]
    cumulative = jnp.cumsum(log_decay, axis=1)
    block = cumulative.shape[1]
    indices = jnp.arange(block)
    causal = (indices[:, None] >= indices[None, :])[None, :, :]
    spread = cumulative[:, :, None] - cumulative[:, None, :]
    weights = jnp.where(causal, jnp.exp(jnp.where(causal, spread, 0.0)), 0.0)
    affinity = jnp.dot(c_block, b_block.T, precision=HIGH)
    scores = affinity[None, :, :] * weights * step_block[:, None, :]
    block_out = jnp.einsum("hps,hts->hpt", x_block, scores, precision=HIGH)
    block_out = block_out + jnp.exp(cumulative)[:, None, :] * jnp.einsum(
        "hpn,tn->hpt", carried, c_block, precision=HIGH
    )
    tail_weight = jnp.exp(cumulative[:, -1:] - cumulative) * step_block
    updated = jnp.exp(cumulative[:, -1])[:, None, None] * carried
    updated = updated + jnp.einsum(
        "hps,sn->hpn", x_block * tail_weight[:, None, :], b_block, precision=HIGH
    )
    return (updated, block_out)


def sweep(streams, b_rows, c_rows, dt_rows, alog_part, skip_part, state_in):
    head_count, head_width, length = streams.shape
    blocks = length // SPAN
    step_size = jax.nn.softplus(dt_rows)
    decay_rate = -jnp.exp(alog_part)
    x_blocks = streams.reshape(head_count, head_width, blocks, SPAN).transpose(2, 0, 1, 3)
    b_blocks = b_rows.reshape(blocks, SPAN, b_rows.shape[1])
    c_blocks = c_rows.reshape(blocks, SPAN, c_rows.shape[1])
    s_blocks = step_size.reshape(head_count, blocks, SPAN).transpose(1, 0, 2)

    def advance(carried, inputs):
        return span_pass(carried, inputs[0], inputs[1], inputs[2], inputs[3], decay_rate)

    state_end, outputs = lax.scan(advance, state_in, (x_blocks, b_blocks, c_blocks, s_blocks))
    mixed_f = outputs.transpose(1, 2, 0, 3).reshape(head_count, head_width, length)
    return (mixed_f + skip_part[:, None, None] * streams, state_end)


def per_device(head_inputs, b_proj, c_proj, dt_raw, a_log, d_skip, w_out, out_grad):
    head_count = dt_raw.shape[1]
    length = head_inputs.shape[2]
    head_width = head_inputs.shape[1] // head_count
    streams = head_inputs[0].astype(jnp.float32).reshape(head_count, head_width, length)
    b_rows = b_proj[0].astype(jnp.float32)
    c_rows = c_proj[0].astype(jnp.float32)
    dt_rows = dt_raw[0]
    decay_rate = -jnp.exp(a_log)
    step_size = jax.nn.softplus(dt_rows)
    cumulative = jnp.cumsum(step_size * decay_rate[:, None], axis=1)
    device_decay = cumulative[:, -1]
    tail_weight = jnp.exp(device_decay[:, None] - cumulative) * step_size
    local_state = jnp.einsum(
        "hpt,tn->hpn", streams * tail_weight[:, None, :], b_rows, precision=HIGH
    )
    totals = lax.all_gather(device_decay[None, :], "seq", axis=0, tiled=True)
    prefix = jnp.cumsum(totals, axis=0)
    my_index = lax.axis_index("seq")
    reached = lax.dynamic_index_in_dim(prefix, my_index, 0, keepdims=False)
    before = reached - device_decay
    shard_part = lax.all_gather(local_state[None], "seq", axis=0, tiled=True)
    row_count = shard_part.shape[0]
    indices = jnp.arange(row_count, dtype=jnp.int32)
    prefix_ends = prefix
    active = (indices < my_index)[:, None]
    weights = jnp.where(active, jnp.exp(jnp.where(active, before[None, :] - prefix_ends, 0.0)), 0.0)
    state_in = jnp.einsum("jh,jhpn->hpn", weights, shard_part, precision=HIGH)

    def local_sweep(xa, ba, ca, da, aa, sa):
        return sweep(xa, ba, ca, da, aa, sa, state_in)

    primal, pullback = jax.vjp(local_sweep, streams, b_rows, c_rows, dt_rows, a_log, d_skip)
    mixed_half = primal[0].reshape(head_count * head_width, length).astype(jnp.bfloat16)
    g_full = lax.all_gather(out_grad[0], "tensor", axis=0, tiled=True)
    cotan_sum = jnp.dot(
        lax.all_gather(w_out, "dp", axis=1, tiled=True), g_full, preferred_element_type=jnp.float32
    )
    cotan_half = cotan_sum.astype(jnp.bfloat16)
    y_cotan = (
        lax.optimization_barrier(cotan_half)
        .astype(jnp.float32)
        .reshape(head_count, head_width, length)
    )
    local_cotan = jnp.einsum(
        "hpt,tn->hpn", y_cotan * jnp.exp(cumulative)[:, None, :], c_rows, precision=HIGH
    )
    shard_part = lax.all_gather(local_cotan[None], "seq", axis=0, tiled=True)
    row_count = shard_part.shape[0]
    indices = jnp.arange(row_count, dtype=jnp.int32)
    prefix_ends = prefix
    active = (indices > my_index)[:, None]
    weights = jnp.where(
        active, jnp.exp(jnp.where(active, prefix_ends - totals - reached[None, :], 0.0)), 0.0
    )
    cotan_in = jnp.einsum("jh,jhpn->hpn", weights, shard_part, precision=HIGH)
    grads = pullback((y_cotan, cotan_in))
    w_terms = lax.dot_general(
        mixed_half, g_full, (((1,), (1,)), ((), ())), preferred_element_type=jnp.float32
    )
    grad_w = lax.psum_scatter(w_terms, ("seq", "dp"), scatter_dimension=1, tiled=True).astype(
        jnp.bfloat16
    )
    grad_b, grad_c = lax.psum((grads[1], grads[2]), "tensor")
    grad_alog, grad_skip = lax.psum((grads[4], grads[5]), ("seq", "dp"))
    grad_inputs = grads[0].reshape(head_count * head_width, length).astype(jnp.bfloat16)
    return (
        mixed_half[None],
        grad_inputs[None],
        grad_b.astype(jnp.bfloat16)[None],
        grad_c.astype(jnp.bfloat16)[None],
        grads[3][None],
        grad_alog,
        grad_skip,
        grad_w,
    )


def solution(mesh):
    in_specs = (
        P("dp", "tensor", "seq"),
        P("dp", "seq", None),
        P("dp", "seq", None),
        P("dp", "tensor", "seq"),
        P("tensor"),
        P("tensor"),
        P("tensor", "dp"),
        P("dp", "tensor", "seq"),
    )
    out_specs = (
        P("dp", "tensor", "seq"),
        P("dp", "tensor", "seq"),
        P("dp", "seq", None),
        P("dp", "seq", None),
        P("dp", "tensor", "seq"),
        P("tensor"),
        P("tensor"),
        P("tensor", ("seq", "dp")),
    )
    return jax.shard_map(
        per_device, mesh=mesh, in_specs=in_specs, out_specs=out_specs, check_vma=False
    )
```

profile of v0, /device:TPU:16, one launch (start us, length us, event | category | flops | bytes accessed | tf_op | source)
XLA Modules:
  0.0 658.8 jit_solution(519363650831749236)
XLA Ops:
  10.1 1.5 reduce-window.46
  15.4 17.3 %all-gather.9.cloned.1.call-done = bf16[320,2560]{1,0:T(8,128)(2,1)} async-done(((bf16[320,1280]{1,0:T(8,128)(2,1)}), bf16[320,2560]{1,0:T(8,128)(2,1)}) %all-gather.9.cloned.1.call-update) | async-done | bytes 1638416 | tf_op jit(solution)/shard_map/all_gather | solution.py:86
  32.7 47.4 %all-gather.13.cloned.1.call-done = bf16[1,2560,512]{2,1,0:T(8,128)(2,1)} async-done(((bf16[1,320,512]{2,1,0:T(8,128)(2,1)}), bf16[1,2560,512]{2,1,0:T(8,128)(2,1)}) %all-gather.13.cloned.1.call-update) | async-done | bytes 2621456 | tf_op jit(solution)/shard_map/all_gather | solution.py:84
  80.0 3.2 fusion.131
  87.3 76.9 %all-reduce.2 = f32[160]{0:T(256)S(1)} all-reduce(f32[160]{0:T(256)S(1)} %dynamic-update-slice), channel_id=2, replica_groups=mesh['seq'=32,'dp'=2,'tensor'=8] {'seq'}, use_global_device_ids=true, to_apply=%add.2 | all-reduce | flops 160 | bytes 1280
  167.5 7.2 %all-gather.11.cloned.1.call-done = f32[160,64,128]{2,1,0:T(8,128)} async-done(((f32[5,64,128]{2,1,0:T(8,128)}), f32[160,64,128]{2,1,0:T(8,128)}) %all-gather.11.cloned.1.call-update) | async-done | bytes 5242896 | tf_op jit(solution)/shard_map/all_gather | solution.py:71
  174.6 7.7 %fusion.125 = f32[5,1,64,128]{3,1,2,0:T(1,128)S(1)} fusion(f32[32,5,1,1]{0,2,3,1:T(1,128)S(1)} %copy.117, f32[32,5,64,128]{3,2,1,0:T(8,128)} %bitcast.487), kind=kOutput, calls=%fused_computation.159 | convolution fusion | flops 15728640 | bytes 5407360 | tf_op jit(solution)/shard_map/jh,jhpn->hpn/dot_general | solution.py:77
  185.1 23.1 %while.75 = (s32[]{:T(128)}, f32[5,64,128]{2,1,0:T(8,128)S(1)}, f32[2,5,64,256]{3,2,1,0:T(8,128)}, f32[2,5,256,256]{3,2,1,0:T(8,128)}, f32[2,128,256]{1,2,0:T(8,...) while((s32[]{:T(128)}, f32[5,64,128]{2,1,0:T(8,128)S(1)}, ...), condition=%wide.region_6.7_spmd.clone.clone, body=%wide.region_3.6_spmd.clone.clone.sunk | while | flops 607838976 | bytes 16159797 | solution.py:45
  185.2 1.5 reduce-window.60
  188.2 2.8 multiply_dynamic-update-slice_fusion.4
  192.4 2.4 fusion.212
  196.8 1.5 reduce-window.60
  199.8 2.8 multiply_dynamic-update-slice_fusion.4
  204.0 2.4 fusion.212
  208.2 1.6 copy.110
  211.3 5.4 fusion.127
  217.6 48.0 %all-gather.15.cloned.1.call-done = f32[160,64,128]{2,1,0:T(8,128)} async-done(((f32[5,64,128]{2,1,0:T(8,128)}), f32[160,64,128]{2,1,0:T(8,128)}) %all-gather.15.cloned.1.call-update) | async-done | bytes 5242896 | tf_op jit(solution)/shard_map/all_gather | solution.py:97
  265.6 7.7 %fusion.123 = f32[5,1,64,128]{3,1,2,0:T(1,128)S(1)} fusion(f32[32,5,1,1]{0,2,3,1:T(1,128)S(1)} %copy.120, f32[32,5,64,128]{3,2,1,0:T(8,128)} %bitcast.486), kind=kOutput, calls=%fused_computation.157 | convolution fusion | flops 15728640 | bytes 5407360 | tf_op jit(solution)/shard_map/jh,jhpn->hpn/dot_general | solution.py:105
  275.7 46.3 %while.76 = (s32[]{:T(128)}, f32[5]{0:T(128)S(1)}, f32[5,64,128]{2,1,0:T(8,128)S(1)}, f32[2,5,64,256]{3,2,1,0:T(8,128)}, f32[2,256,128]{2,1,0:T(8,128)}, /*index...) while((s32[]{:T(128)}, f32[5]{0:T(128)S(1)}, ...), condition=%wide.region_19.20_spmd.clone.clone, body=%wide.region_7.19_spmd.clone.clone.sunk | while | flops 1212566272 | bytes 13529267 | solution.py:45
  276.7 3.9 fusion.227
  282.7 6.3 reduce-window.62
  290.2 1.9 fusion.240
  292.4 1.8 convolution_bitcast_fusion.5
  295.4 3.0 fusion.238
  299.9 3.9 fusion.227
  305.9 6.3 reduce-window.62
  313.4 1.9 fusion.240
  315.5 1.8 convolution_bitcast_fusion.5
  318.6 3.0 fusion.238
  322.1 1.6 copy.114
  325.6 290.5 %all-reduce.8 = (f32[5]{0:T(128)}, f32[5]{0:T(128)}, bf16[320,2560]{0,1:T(8,128)(2,1)S(1)}) all-reduce(f32[5]{0:T(128)S(1)} %negate_multiply_fusion, f32[5]{0:T(128)S(1)} %reduce_sum.212, f32[320,2560]{0,1:T(8,128)} %fusion.127), channel_id=1, replica_groups=mesh['seq'=32,'dp'=2,'tensor'=8] {'seq','dp'}, use_global_device_ids=true, to_apply=%region_22.23 | all-reduce | flops 819210 | bytes 4915280 | tf_op jit(solution)/shard_map/psum | solution.py:114
  616.8 35.5 %all-reduce.9 = (bf16[512,128]{1,0:T(8,128)(2,1)}, bf16[512,128]{1,0:T(8,128)(2,1)}) all-reduce(f32[512,128]{1,0:T(8,128)S(1)} %bitcast.502, f32[512,128]{1,0:T(8,128)S(1)} %bitcast.503), channel_id=1, replica_groups=mesh['seq'=32,'dp'=2,'tensor'=8] {'tensor'}, use_global_device_ids=true, to_apply=%region_20.21 | all-reduce | flops 131072 | bytes 786432 | tf_op jit(solution)/shard_map/psum | solution.py:113
  (224 shorter events, 44.2 us)
Async XLA Ops:
  7.2 7.0 %copy-start.8 = (bf16[1,512,128]{2,1,0:T(8,128)(2,1)S(1)}, bf16[1,512,128]{2,1,0:T(8,128)(2,1)}, u32[]{:S(2)}) copy-start(bf16[1,512,128]{2,1,0:T(8,128)(2,1)} %param.13) | copy-start | bytes 393220
  7.2 25.5 %all-gather.9.cloned.1.call-start = ((), (), s32[]{:S(2)}) async-start(), calls=%async_computation | async-start | bytes 2457600 | tf_op jit(solution)/shard_map/all_gather | solution.py:86
  7.9 72.1 %all-gather.13.cloned.1.call-start = ((), (), s32[]{:S(2)}) async-start(), calls=%async_computation.2 | async-start | bytes 2949120 | tf_op jit(solution)/shard_map/all_gather | solution.py:84
  8.7 166.0 %all-gather.11.cloned.1.call-start = ((), (), s32[]{:S(2)}) async-start(), calls=%async_computation.1 | async-start | bytes 5406720 | tf_op jit(solution)/shard_map/all_gather | solution.py:71
  15.3 68.1 %copy-start.9 = (bf16[1,512,128]{2,1,0:T(8,128)(2,1)S(1)}, bf16[1,512,128]{2,1,0:T(8,128)(2,1)}, u32[]{:S(2)}) copy-start(bf16[1,512,128]{2,1,0:T(8,128)(2,1)} %param.14) | copy-start | bytes 393220
  15.3 69.2 %copy-start = (bf16[1,320,512]{2,1,0:T(8,128)(2,1)S(1)}, bf16[1,320,512]{2,1,0:T(8,128)(2,1)}, u32[]{:S(2)}) copy-start(bf16[1,320,512]{2,1,0:T(8,128)(2,1)} %param.12) | copy-start | bytes 983044
  15.3 250.2 %all-gather.15.cloned.1.call-start = ((), (), s32[]{:S(2)}) async-start(), calls=%async_computation.3 | async-start | bytes 5406720 | tf_op jit(solution)/shard_map/all_gather | solution.py:97
  83.3 83.7 %copy-start.3 = (bf16[320,512]{1,0:T(8,128)(2,1)}, bf16[320,512]{1,0:T(8,128)(2,1)S(1)}, u32[]{:S(2)}) copy-start(bf16[320,512]{1,0:T(8,128)(2,1)S(1)} %fusion.131) | copy-start | bytes 983044
  83.3 81.4 %copy-start.10 = (f32[1,5,512]{2,0,1:T(1,128)S(1)}, f32[1,5,512]{2,0,1:T(1,128)}, u32[]{:S(2)}) copy-start(f32[1,5,512]{2,0,1:T(1,128)} %param.15) | copy-start | bytes 30724
  83.3 81.6 %copy-start.11 = (f32[5]{0:T(128)S(1)}, f32[5]{0:T(128)}, u32[]{:S(2)}) copy-start(f32[5]{0:T(128)} %param.17) | copy-start | bytes 64
  191.2 3.7 copy-start.1
  194.9 0.8 copy-start.2
  202.8 3.6 copy-start.1
  206.4 0.8 copy-start.2
  211.3 5.4 copy-start.5
  322.0 1.7 copy-start.4
  322.0 2.7 copy-start.12
  323.8 293.0 %copy-start.6 = (f32[2,256,128]{2,1,0:T(8,128)S(1)}, f32[2,256,128]{2,1,0:T(8,128)}, u32[]{:S(2)}) copy-start(f32[2,256,128]{2,1,0:T(8,128)} %get-tuple-element.972) | copy-start | bytes 786436
  323.8 293.0 %copy-start.7 = (f32[2,256,128]{2,1,0:T(8,128)S(1)}, f32[2,256,128]{2,1,0:T(8,128)}, u32[]{:S(2)}) copy-start(f32[2,256,128]{2,1,0:T(8,128)} %get-tuple-element.973) | copy-start | bytes 786436
Sparse Core Ops, SparseCore 0:
  10.1 22.5 all-gather.8
  34.7 45.2 all-gather.12
  83.8 90.8 all-gather.10
  177.7 87.8 all-gather.14
where the time goes:
time: 660 us; the launch traced here: 659 us
  blocking collectives  403 us (61%)
  waiting for transfers between devices  121 us (18%)
  matrix products  63.7 us (10%)
  other arithmetic  33.6 us (5%)
  local copies, waits for them, and re-layouts  21.4 us (3%)
  between operations  15.6 us (2%)
    psum x1, blocking collectives, per_device(): grad_alog, grad_skip = lax.psum((grads[4], grads[5]), ('seq', 'dp'))  291 us
    unnamed x1, blocking collectives  76.9 us
    all_gather x1, waiting for transfers between devices, per_device(): shard_part = lax.all_gather(local_cotan[None], 'seq', axis=0, tiled=True)  48 us
    all_gather x1, waiting for transfers between devices, per_device(): g_full = lax.all_gather(out_grad[0], 'tensor', axis=0, tiled=True)  47.4 us
    psum x1, blocking collectives, per_device(): grad_b, grad_c = lax.psum((grads[1], grads[2]), 'tensor')  35.5 us
    dot_general x6, matrix products, span_pass(): block_out = jnp.einsum('hps,hts->hpt', x_block, scores, precision=HIGH)  18.5 us
    another operation x23, other arithmetic  17.6 us
    all_gather x1, waiting for transfers between devices, per_device(): lax.all_gather(w_out, 'dp', axis=1, tiled=True)  17.3 us
  transfers between devices with their start and end apart: 4, of which 4 were waited for; matrix products, arithmetic and copies ran while one was open for 9% of the time, Pallas kernels for 0%

commit v1 on v0

--- a/solution.py
+++ b/solution.py
@@ -81,7 +81,9 @@
 
     primal, pullback = jax.vjp(local_sweep, streams, b_rows, c_rows, dt_rows, a_log, d_skip)
     mixed_half = primal[0].reshape(head_count * head_width, length).astype(jnp.bfloat16)
-    g_full = lax.all_gather(out_grad[0], "tensor", axis=0, tiled=True)
+    g_full = jnp.concatenate(
+        lax.all_to_all(jnp.stack([out_grad[0]] * lax.axis_size("tensor")), "tensor", 0, 0), axis=0
+    )
     cotan_sum = jnp.dot(
         lax.all_gather(w_out, "dp", axis=1, tiled=True), g_full, preferred_element_type=jnp.float32
     )

time: 660 us -> 617 us (0.935)
  the two profiles are of different devices: /device:TPU:16 before, /device:TPU:8 now
where the time goes in v1:
time: 617 us; the launch traced here: 616 us
  blocking collectives  406 us (66%)
  matrix products  63.7 us (10%)
  waiting for transfers between devices  59.3 us (10%)
  other arithmetic  37.5 us (6%)
  local copies, waits for them, and re-layouts  23.6 us (4%)
  between operations  15.5 us (3%)
  starting transfers between devices  10.2 us (2%)
    psum x1, blocking collectives, per_device(): grad_alog, grad_skip = lax.psum((grads[4], grads[5]), ('seq', 'dp'))  291 us
    unnamed x1, blocking collectives  81.4 us
    all_to_all x1, waiting for transfers between devices, per_device(): lax.all_to_all(jnp.stack([out_grad[0]] * lax.axis_size('tensor')), 'tenso...  52.2 us
    psum x1, blocking collectives, per_device(): grad_b, grad_c = lax.psum((grads[1], grads[2]), 'tensor')  34.1 us
    dot_general x6, matrix products, span_pass(): block_out = jnp.einsum('hps,hts->hpt', x_block, scores, precision=HIGH)  18.5 us
    another operation x23, other arithmetic  17.6 us
  transfers between devices with their start and end apart: 4, of which 2 were waited for; matrix products, arithmetic and copies ran while one was open for 10% of the time, Pallas kernels for 0%

profile of v1, /device:TPU:8, one launch (start us, length us, event | category | flops | bytes accessed | tf_op | source)
XLA Modules:
  0.0 615.9 jit_solution(12326886181294547622)
XLA Ops:
  9.4 1.5 reduce-window.46
  14.6 1.7 stack.3
  16.3 10.1 %all-to-all-start = ((bf16[8,320,512]{2,1,0:T(8,128)(2,1)}), bf16[8,320,512]{2,1,0:T(8,128)(2,1)}, u32[]{:S(2)}, u32[]{:S(2)}) async-start(bf16[8,320,512]{2,1,0:T(8,128)(2,1)} %stack.3), calls=%async_computation | async-start | bytes 5242880 | tf_op jit(solution)/shard_map/all_to_all | solution.py:85
  26.4 6.3 %all-gather.7.cloned.1.call-done = bf16[320,2560]{1,0:T(8,128)(2,1)} async-done(((bf16[320,1280]{1,0:T(8,128)(2,1)}), bf16[320,2560]{1,0:T(8,128)(2,1)}) %all-gather.7.cloned.1.call-update) | async-done | bytes 1638416 | tf_op jit(solution)/shard_map/all_gather | solution.py:88
  32.7 52.2 %all-to-all-done = bf16[8,320,512]{2,1,0:T(8,128)(2,1)} async-done(((bf16[8,320,512]{2,1,0:T(8,128)(2,1)}), bf16[8,320,512]{2,1,0:T(8,128)(2,1)}, u32[]{:S(2)}, u32[]{:S(2)}) %all-to-all-start) | async-done | bytes 2621472 | tf_op jit(solution)/shard_map/all_to_all | solution.py:85
  85.0 3.3 convolution_convert_fusion
  92.3 81.4 %all-reduce.2 = f32[160]{0:T(256)S(1)} all-reduce(f32[160]{0:T(256)S(1)} %dynamic-update-slice), channel_id=2, replica_groups=mesh['seq'=32,'dp'=2,'tensor'=8] {'seq'}, use_global_device_ids=true, to_apply=%add.2 | all-reduce | flops 160 | bytes 1280
  178.9 7.7 %fusion.125 = f32[5,1,64,128]{3,1,2,0:T(1,128)S(1)} fusion(f32[32,5,1,1]{0,2,3,1:T(1,128)S(1)} %copy.121, f32[32,5,64,128]{3,2,1,0:T(8,128)} %bitcast.480), kind=kOutput, calls=%fused_computation.159 | convolution fusion | flops 15728640 | bytes 5407360 | tf_op jit(solution)/shard_map/jh,jhpn->hpn/dot_general | solution.py:77
  189.3 24.0 %while.75 = (s32[]{:T(128)}, f32[5,64,128]{2,1,0:T(8,128)S(1)}, f32[2,5,64,256]{3,2,1,0:T(8,128)}, f32[2,5,256,256]{3,2,1,0:T(8,128)}, f32[2,128,256]{1,2,0:T(8,...) while((s32[]{:T(128)}, f32[5,64,128]{2,1,0:T(8,128)S(1)}, ...), condition=%wide.region_6.7_spmd.clone.clone, body=%wide.region_3.6_spmd.clone.clone.sunk | while | flops 607838976 | bytes 10914297 | solution.py:45
  189.4 1.5 reduce-window.60
  192.4 2.8 multiply_dynamic-update-slice_fusion.4
  196.6 2.4 fusion.205
  201.4 1.5 reduce-window.60
  204.4 2.9 multiply_dynamic-update-slice_fusion.4
  208.7 2.4 fusion.205
  215.0 5.3 fusion.145
  222.2 2.0 add_convert_fusion.2
  224.1 7.7 %fusion.123 = f32[5,1,64,128]{3,1,2,0:T(1,128)S(1)} fusion(f32[32,5,1,1]{0,2,3,1:T(1,128)S(1)} %copy.124, f32[32,5,64,128]{3,2,1,0:T(8,128)} %bitcast.479), kind=kOutput, calls=%fused_computation.157 | convolution fusion | flops 15728640 | bytes 5407360 | tf_op jit(solution)/shard_map/jh,jhpn->hpn/dot_general | solution.py:107
  234.3 46.3 %while.76 = (s32[]{:T(128)}, f32[5]{0:T(128)S(1)}, f32[5,64,128]{2,1,0:T(8,128)S(1)}, f32[2,5,64,256]{3,2,1,0:T(8,128)}, f32[2,256,128]{2,1,0:T(8,128)}, /*index...) while((s32[]{:T(128)}, f32[5]{0:T(128)S(1)}, ...), condition=%wide.region_19.20_spmd.clone.clone, body=%wide.region_7.19_spmd.clone.clone.sunk | while | flops 1212566272 | bytes 13529267 | solution.py:45
  235.3 3.9 fusion.220
  241.3 6.3 %reduce-window.62 = f32[5,2,128]{2,1,0:T(2,128)S(1)} reduce-window(f32[5,2,128]{2,1,0:T(2,128)S(1)} %reshape.778, f32[]{:T(128)} %constant.173.clone.1..sunk.1), window={size=1x1x128 pad=0_0x0_0x0_127}, to_apply=%region_14.14 | reduce-window | flops 162560 | bytes 10244 | tf_op jit(solution)/shard_map/reduce-window.20
  248.8 1.9 fusion.233
  251.0 1.8 convolution_bitcast_fusion.5
  254.0 2.9 fusion.231
  258.4 3.9 fusion.220
  264.4 6.3 %reduce-window.62 = f32[5,2,128]{2,1,0:T(2,128)S(1)} reduce-window(f32[5,2,128]{2,1,0:T(2,128)S(1)} %reshape.778, f32[]{:T(128)} %constant.173.clone.1..sunk.1), window={size=1x1x128 pad=0_0x0_0x0_127}, to_apply=%region_14.14 | reduce-window | flops 162560 | bytes 10244 | tf_op jit(solution)/shard_map/reduce-window.20
  272.0 1.9 fusion.233
  274.1 1.8 convolution_bitcast_fusion.5
  277.1 3.0 fusion.231
  280.6 1.6 copy.117
  284.2 290.5 %all-reduce.8 = (f32[5]{0:T(128)}, f32[5]{0:T(128)}, bf16[320,2560]{0,1:T(8,128)(2,1)S(1)}) all-reduce(f32[5]{0:T(128)S(1)} %negate_multiply_fusion, f32[5]{0:T(128)S(1)} %reduce_sum.212, f32[320,2560]{0,1:T(8,128)} %fusion.145), channel_id=1, replica_groups=mesh['seq'=32,'dp'=2,'tensor'=8] {'seq','dp'}, use_global_device_ids=true, to_apply=%region_22.23 | all-reduce | flops 819210 | bytes 4915280 | tf_op jit(solution)/shard_map/psum | solution.py:116
  575.3 34.1 %all-reduce.9 = (bf16[512,128]{1,0:T(8,128)(2,1)}, bf16[512,128]{1,0:T(8,128)(2,1)}) all-reduce(f32[512,128]{1,0:T(8,128)S(1)} %bitcast.495, f32[512,128]{1,0:T(8,128)S(1)} %bitcast.496), channel_id=1, replica_groups=mesh['seq'=32,'dp'=2,'tensor'=8] {'tensor'}, use_global_device_ids=true, to_apply=%region_20.21 | all-reduce | flops 131072 | bytes 786432 | tf_op jit(solution)/shard_map/psum | solution.py:115
  (222 shorter events, 47.5 us)
Async XLA Ops:
  7.2 6.3 %copy-start.7 = (bf16[1,512,128]{2,1,0:T(8,128)(2,1)S(1)}, bf16[1,512,128]{2,1,0:T(8,128)(2,1)}, u32[]{:S(2)}) copy-start(bf16[1,512,128]{2,1,0:T(8,128)(2,1)} %param.13) | copy-start | bytes 393220
  7.2 7.4 %copy-start.9 = (bf16[1,320,512]{2,1,0:T(8,128)(2,1)S(1)}, bf16[1,320,512]{2,1,0:T(8,128)(2,1)}, u32[]{:S(2)}) copy-start(bf16[1,320,512]{2,1,0:T(8,128)(2,1)} %param.19) | copy-start | bytes 983044
  7.2 25.6 %all-gather.7.cloned.1.call-start = ((), (), s32[]{:S(2)}) async-start(), calls=%async_computation.1 | async-start | bytes 2457600 | tf_op jit(solution)/shard_map/all_gather | solution.py:88
  7.9 170.9 %all-gather.9.cloned.1.call-start = ((), (), s32[]{:S(2)}) async-start(), calls=%async_computation.2 | async-start | bytes 5406720 | tf_op jit(solution)/shard_map/all_gather | solution.py:71
  16.3 68.6 %all-to-all-start = ((bf16[8,320,512]{2,1,0:T(8,128)(2,1)}), bf16[8,320,512]{2,1,0:T(8,128)(2,1)}, u32[]{:S(2)}, u32[]{:S(2)}) async-start(bf16[8,320,512]{2,1,0:T(8,128)(2,1)} %stack.3), calls=%async_computation | async-start | bytes 5242880 | tf_op jit(solution)/shard_map/all_to_all | solution.py:85
  26.4 197.7 %all-gather.11.cloned.1.call-start = ((), (), s32[]{:S(2)}) async-start(), calls=%async_computation.3 | async-start | bytes 5406720 | tf_op jit(solution)/shard_map/all_gather | solution.py:99
  85.0 3.4 copy-start.8
  85.0 4.6 copy-start.1
  88.3 88.2 %copy-start.3 = (bf16[320,512]{1,0:T(8,128)(2,1)}, bf16[320,512]{1,0:T(8,128)(2,1)S(1)}, u32[]{:S(2)}) copy-start(bf16[320,512]{1,0:T(8,128)(2,1)S(1)} %convolution_convert_fusion) | copy-start | bytes 983044
  88.3 85.9 %copy-start.10 = (f32[1,5,512]{2,0,1:T(1,128)S(1)}, f32[1,5,512]{2,0,1:T(1,128)}, u32[]{:S(2)}) copy-start(f32[1,5,512]{2,0,1:T(1,128)} %param.15) | copy-start | bytes 30724
  88.3 86.1 %copy-start.11 = (f32[5]{0:T(128)S(1)}, f32[5]{0:T(128)}, u32[]{:S(2)}) copy-start(f32[5]{0:T(128)} %param.17) | copy-start | bytes 64
  215.0 5.3 copy-start
  220.3 1.9 copy-start.2
  280.6 1.7 copy-start.4
  280.6 2.7 copy-start.12
  282.3 293.0 %copy-start.5 = (f32[2,256,128]{2,1,0:T(8,128)S(1)}, f32[2,256,128]{2,1,0:T(8,128)}, u32[]{:S(2)}) copy-start(f32[2,256,128]{2,1,0:T(8,128)} %get-tuple-element.972) | copy-start | bytes 786436
  282.3 293.0 %copy-start.6 = (f32[2,256,128]{2,1,0:T(8,128)S(1)}, f32[2,256,128]{2,1,0:T(8,128)}, u32[]{:S(2)}) copy-start(f32[2,256,128]{2,1,0:T(8,128)} %get-tuple-element.973) | copy-start | bytes 786436
Sparse Core Ops, SparseCore 0:
  10.1 22.5 all-gather.6
  36.5 92.1 all-gather.8
  131.9 87.5 all-gather.10
